TPU v7x, 1024 devices: a whole 4x8x16 slice. The times are simulated.
1024 devices in a mesh: dp: 8 (over y), expert: 32 (over z, core), tensor: 4 (over x).
Axes of the slice: x: 4, y: 8, z: 16, core: 2. Of those that a mesh axis runs over, the one named last changes fastest.
Arguments:
- out_grad: bfloat16 [32768, 3584], P(('dp', 'expert'), 'tensor'), may hold values from -6 to 6
- route_ids: int32 [32768, 2], P(('dp', 'expert')), may hold values from 0 to 31, all different within a row; in each aligned block of 128 rows (0 to 127, 128 to 255, ...) at most 12 rows name the same one
- route_probs: float32 [32768, 2], P(('dp', 'expert')), may hold values from 0.2 to 1
- dense_gate_pre: bfloat16 [32768, 2432], P(('dp', 'expert'), 'tensor'), may hold values from -6 to 6
- dense_up_pre: bfloat16 [32768, 2432], P(('dp', 'expert'), 'tensor'), may hold values from -6 to 6
- dense_down: bfloat16 [2432, 3584], P('tensor', ('dp', 'expert')), may hold values from -0.09375 to 0.09375
- expert_gate_pre: bfloat16 [8, 32, 384, 2432], P('dp', 'expert', None, 'tensor'), may hold values from -6 to 6
- expert_up_pre: bfloat16 [8, 32, 384, 2432], P('dp', 'expert', None, 'tensor'), may hold values from -6 to 6
- expert_down: bfloat16 [32, 2432, 3584], P('expert', 'tensor'), may hold values from -0.09375 to 0.09375
Outputs:
- dense_gate_grad: bfloat16 [32768, 2432], P(('dp', 'expert'), 'tensor')
- dense_up_grad: bfloat16 [32768, 2432], P(('dp', 'expert'), 'tensor')
- expert_gate_grad: bfloat16 [8, 32, 384, 2432], P('dp', 'expert', None, 'tensor')
- expert_up_grad: bfloat16 [8, 32, 384, 2432], P('dp', 'expert', None, 'tensor')
Inputs may be any that keep to these rules, and one draw needn't show every extreme that they name: `route_ids`: each row names 2 different experts. In the rows of one device no expert is named more than 12 times, a bound that some block reaches.
All inputs are finite; a program needn't handle non-finite values.
Results may differ from a plain program's by a relative error of at most 0.0049.
Values may be sent and summed in bfloat16 or wider, within the bound.
A program may use at most 64 MiB of HBM per device.

v0:
```python
import jax
import jax.numpy as jnp
from jax import lax
from jax.sharding import PartitionSpec as P


def slot_table(route_ids, route_probs, experts, capacity, slot_count):
    width = route_ids.shape[1]
    flat_ids = route_ids.reshape(-1)
    flat_probs = route_probs.reshape(-1)
    total_rows = flat_ids.shape[0]
    onehot = (flat_ids[:, None] == jnp.arange(experts, dtype=jnp.int32)[None, :]).astype(jnp.int32)
    earlier = jnp.cumsum(onehot, axis=0) - onehot
    position = jnp.sum(earlier * onehot, axis=1)
    slot_cell = flat_ids * capacity + position
    targets = (
        jnp.arange(experts, dtype=jnp.int32)[:, None] * capacity
        + jnp.arange(slot_count, dtype=jnp.int32)[None, :]
    ).reshape(-1)
    matches = targets[:, None] == slot_cell[None, :]
    token_of = jnp.arange(total_rows, dtype=jnp.int32) // width
    row_scale = jnp.sum(jnp.where(matches, flat_probs[None, :], jnp.float32(0.0)), axis=1)
    owner_row = jnp.sum(jnp.where(matches, token_of[None, :], 0), axis=1)
    return (owner_row, row_scale)


def swiglu_back(gate_pre, up_pre, hidden):
    gate_val = gate_pre.astype(jnp.float32)
    up_val = up_pre.astype(jnp.float32)
    sigma = jax.nn.sigmoid(gate_val)
    up_grad = hidden * gate_val * sigma
    gate_grad = hidden * up_val * sigma * (1.0 + gate_val * (1.0 - sigma))
    return (gate_grad.astype(jnp.bfloat16), up_grad.astype(jnp.bfloat16))


def local(
    out_grad,
    route_ids,
    route_probs,
    dense_gate_pre,
    dense_up_pre,
    dense_down,
    expert_gate_pre,
    expert_up_pre,
    expert_down,
):
    experts = lax.axis_size("expert")
    capacity = expert_gate_pre.shape[2] // experts
    full_grad = lax.all_gather(out_grad, "tensor", axis=1, tiled=True)
    dense_hidden = lax.dot_general(
        full_grad,
        lax.all_gather(dense_down, ("dp", "expert"), axis=1, tiled=True),
        (((1,), (1,)), ((), ())),
        preferred_element_type=jnp.float32,
    )
    dense_gate_grad, dense_up_grad = swiglu_back(dense_gate_pre, dense_up_pre, dense_hidden)
    weight = expert_down[0]
    owner_row, row_scale = slot_table(route_ids, route_probs, experts, capacity, capacity)
    sent_rows = jnp.take(out_grad, owner_row, axis=0).astype(jnp.float32) * row_scale[:, None]
    sent_rows = sent_rows.astype(jnp.bfloat16).reshape(experts, capacity, out_grad.shape[1])
    arrived = lax.all_to_all(sent_rows, "expert", split_axis=0, concat_axis=0, tiled=True)
    arrived = arrived.reshape(experts * capacity, out_grad.shape[1])
    hidden = lax.dot_general(
        lax.all_gather(arrived, "tensor", axis=1, tiled=True),
        weight,
        (((1,), (1,)), ((), ())),
        preferred_element_type=jnp.float32,
    )
    expert_gate_grad, expert_up_grad = swiglu_back(
        expert_gate_pre[0, 0], expert_up_pre[0, 0], hidden
    )
    expert_gate_grad = expert_gate_grad.reshape(expert_gate_pre.shape)
    expert_up_grad = expert_up_grad.reshape(expert_up_pre.shape)
    return (dense_gate_grad, dense_up_grad, expert_gate_grad, expert_up_grad)


def solution(mesh):
    placed = (
        P(("dp", "expert"), "tensor"),
        P(("dp", "expert"), None),
        P(("dp", "expert"), None),
        P(("dp", "expert"), "tensor"),
        P(("dp", "expert"), "tensor"),
        P("tensor", ("dp", "expert")),
        P("dp", "expert", None, "tensor"),
        P("dp", "expert", None, "tensor"),
        P("expert", "tensor", None),
    )
    return jax.shard_map(
        local,
        mesh=mesh,
        in_specs=placed,
        out_specs=(
            P(("dp", "expert"), "tensor"),
            P(("dp", "expert"), "tensor"),
            P("dp", "expert", None, "tensor"),
            P("dp", "expert", None, "tensor"),
        ),
        check_vma=False,
    )
```

profile of v0, /device:TPU:1, one launch (start us, length us, event | category | flops | bytes accessed | tf_op | source)
XLA Modules:
  0.0 298.2 jit_solution(7719290337255353987)
XLA Ops:
  7.2 0.8 copy.21
  8.1 0.1 reshape.113
  8.2 0.1 eq.40
  8.4 0.1 add.71
  8.5 0.6 reduce-window.6
  9.1 0.2 slice_reduce_fusion
  9.5 0.2 fusion.13
  9.7 0.1 reduce_sum.33
  9.9 0.8 copy.24
  10.7 0.1 broadcast_in_dim.46
  10.8 0.2 fusion.14
  11.0 0.1 mul.82
  11.1 2.3 gather_fusion
  13.5 0.2 gather.7
  13.6 0.3 multiply_convert_fusion
  13.9 70.4 %all_to_all.5 = bf16[32,12,896]{2,1,0:T(8,128)(2,1)S(1)} all-to-all(bf16[32,12,896]{2,1,0:T(8,128)(2,1)S(1)} %multiply_convert_fusion), channel_id=1, replica_groups=mesh['dp'=8,'expert'=32,'tensor'=4] {'expert'}, dimensions={0} | all-to-all | bytes 1376256 | tf_op jit(solution)/shard_map/all_to_all | solution.py:61
  84.3 1.1 reshape.115
  85.5 0.7 all-gather.6.cloned.1.call-update
  86.2 12.7 %all_gather.9 = bf16[128,3584]{1,0:T(8,128)(2,1)S(1)} all-gather(bf16[128,896]{1,0:T(8,128)(2,1)S(1)} %copy-done), channel_id=1, replica_groups=mesh['dp'=8,'expert'=32,'tensor'=4] {'tensor'}, dimensions={1}, use_global_device_ids=true | all-gather | bytes 1146880 | tf_op jit(solution)/shard_map/all_gather | solution.py:49
  98.9 24.8 %all-gather.4.cloned.1.call-done = bf16[384,3584]{1,0:T(8,128)(2,1)} async-done(((bf16[384,896]{1,0:T(8,128)(2,1)}), bf16[384,3584]{1,0:T(8,128)(2,1)}) %all-gather.4.cloned.1.call-update) | async-done | bytes 2752528 | tf_op jit(solution)/shard_map/all_gather | solution.py:64
  123.7 6.7 %fusion.11 = (bf16[1,1,384,608]{2,3,1,0:T(8,128)(2,1)}, bf16[1,1,384,608]{2,3,1,0:T(8,128)(2,1)}) fusion(bf16[1,1,384,608]{2,3,1,0:T(8,128)(2,1)S(1)} %copy-done.1, bf16[1,1,384,608]{2,3,1,0:T(8,128)(2,1)S(1)} %copy-done.2, bf16[384,3584]{1,0:T(8,128)(2,1)} %all-gather.4.cloned.1.call-done, bf16[1,608,3584]{2,1,0:T(8,128)(2,1)} %param.17), kind=kOutput, calls=%fused_computation.22 | convolution fusion | flops 1677029376 | bytes 8978432 | tf_op jit(solution)/shard_map/dot_general | solution.py:63
  130.4 147.6 %all-gather.6.cloned.1.call-done = bf16[256,14,608]{2,1,0:T(8,128)(2,1)} async-done(((bf16[1,14,608]{2,1,0:T(8,128)(2,1)}), bf16[256,14,608]{2,1,0:T(8,128)(2,1)}) %all-gather.6.cloned.1.call-update) | async-done | bytes 4358160 | tf_op jit(solution)/shard_map/all_gather | solution.py:52
  278.0 8.5 %reshape.129 = bf16[3584,608]{1,0:T(8,128)(2,1)} reshape(bf16[256,14,608]{2,1,0:T(8,128)(2,1)} %all-gather.6.cloned.1.call-done) | data formatting | bytes 8716288
  286.5 4.9 %fusion.22 = (bf16[128,608]{0,1:T(8,128)(2,1)}, bf16[128,608]{0,1:T(8,128)(2,1)}) fusion(bf16[128,608]{0,1:T(8,128)(2,1)S(1)} %copy-done.3, bf16[128,608]{0,1:T(8,128)(2,1)S(1)} %copy-done.4, bf16[128,3584]{1,0:T(8,128)(2,1)S(1)} %all_gather.9, bf16[3584,608]{1,0:T(8,128)(2,1)} %reshape.129), kind=kOutput, calls=%fused_computation.33 | convolution fusion | flops 559009792 | bytes 5898240 | tf_op jit(solution)/shard_map/dot_general | solution.py:50
  (23 shorter events, 0.4 us)
Async XLA Ops:
  7.2 4.0 %copy-start = (bf16[128,896]{1,0:T(8,128)(2,1)S(1)}, bf16[128,896]{1,0:T(8,128)(2,1)}, u32[]{:S(2)}) copy-start(bf16[128,896]{1,0:T(8,128)(2,1)} %param.9) | copy-start | bytes 688132
  7.2 116.5 %all-gather.4.cloned.1.call-start = ((), (), s32[]{:S(2)}) async-start(), calls=%async_computation.1 | async-start | bytes 3440640 | tf_op jit(solution)/shard_map/all_gather | solution.py:64
  13.4 110.3 %copy-start.1 = (bf16[1,1,384,608]{2,3,1,0:T(8,128)(2,1)S(1)}, bf16[1,1,384,608]{2,3,1,0:T(8,128)(2,1)}, u32[]{:S(2)}) copy-start(bf16[1,1,384,608]{2,3,1,0:T(8,128)(2,1)} %param.15) | copy-start | bytes 1400836
  13.4 110.3 %copy-start.2 = (bf16[1,1,384,608]{2,3,1,0:T(8,128)(2,1)S(1)}, bf16[1,1,384,608]{2,3,1,0:T(8,128)(2,1)}, u32[]{:S(2)}) copy-start(bf16[1,1,384,608]{2,3,1,0:T(8,128)(2,1)} %param.16) | copy-start | bytes 1400836
  85.4 192.5 %all-gather.6.cloned.1.call-start = ((), (), s32[]{:S(2)}) async-start(), calls=%async_computation.2 | async-start | bytes 5263360 | tf_op jit(solution)/shard_map/all_gather | solution.py:52
  130.4 156.1 %copy-start.3 = (bf16[128,608]{0,1:T(8,128)(2,1)S(1)}, bf16[128,608]{0,1:T(8,128)(2,1)}, u32[]{:S(2)}) copy-start(bf16[128,608]{0,1:T(8,128)(2,1)} %param.12) | copy-start | bytes 466948
  130.4 156.1 %copy-start.4 = (bf16[128,608]{0,1:T(8,128)(2,1)S(1)}, bf16[128,608]{0,1:T(8,128)(2,1)}, u32[]{:S(2)}) copy-start(bf16[128,608]{0,1:T(8,128)(2,1)} %param.13) | copy-start | bytes 466948
Sparse Core Ops, SparseCore 0:
  85.5 38.1 all-gather.3
  127.9 149.9 all-gather.5
where the time goes:
time: 299 us; the launch traced here: 298 us
  waiting for transfers between devices  173 us (58%)
  blocking collectives  83.1 us (28%)
  local copies, waits for them, and re-layouts  14.6 us (5%)
  between operations  14.2 us (5%)
  matrix products  11.6 us (4%)
    all_gather x1, waiting for transfers between devices, local(): lax.all_gather(dense_down, ('dp', 'expert'), axis=1, tiled=True)  148 us
    all_to_all x1, blocking collectives, local(): lax.all_to_all(sent_rows, 'expert', split_axis=0, concat_axis=0, tiled=True)  70.4 us
    all_gather x1, waiting for transfers between devices, local(): lax.all_gather(arrived, 'tensor', axis=1, tiled=True)  24.8 us
    all_gather x1, blocking collectives, local(): full_grad = lax.all_gather(out_grad, 'tensor', axis=1, tiled=True)  12.7 us
    unnamed x13, local copies, waits for them, and re-layouts  10.2 us
    dot_general x1, matrix products, local(): lax.dot_general(lax.all_gather(arrived, 'tensor', axis=1, tiled=True), we...  6.66 us
  transfers between devices with their start and end apart: 2, of which 2 were waited for; matrix products, arithmetic and copies ran while one was open for 2% of the time, Pallas kernels for 0%

commit v1 on v0

v1 whole, which is shorter than its diff:
```python
import functools

import jax
import jax.numpy as jnp
from jax import lax
from jax.experimental import pallas as pl
from jax.experimental.pallas import tpu as pltpu
from jax.sharding import PartitionSpec as P

MESH = pl.DeviceIdType.MESH
F32 = jnp.float32
BF16 = jnp.bfloat16

Z_GROUPS = ((0, 3), (3, 7), (7, 11), (11, 16))
Z_READY = (1, 3, 5, 8)


def slot_of(offset):
    if offset == 0:
        return 0
    return 2 * offset - 1 if offset > 0 else -2 * offset


def iota(shape, dim):
    return lax.broadcasted_iota(jnp.int32, shape, dim)


def one_hot(mask):
    return jnp.where(mask, 1.0, 0.0).astype(BF16)


def nn(a, b):
    return jnp.dot(a, b, preferred_element_type=F32)


def nt(a, b):
    return lax.dot_general(a, b, (((1,), (1,)), ((), ())), preferred_element_type=F32)


def factors(gate_pre, up_pre):
    a = gate_pre.astype(F32)
    b = up_pre.astype(F32)
    sigma = 1.0 / (1.0 + jnp.exp(-a))
    return b * sigma * (1.0 + a * (1.0 - sigma)), a * sigma


def kernel(
    grad_in, ids_in, probs_in, dgate_in, dup_in, ddown_in, egate_in, eup_in, edown_in,
    dgate_out, dup_out, egate_out, eup_out,
    ids, probs, table, xs, sends, lands, rows, weight, acc, e_gate, e_up, fac_gate, fac_up,
    d_raw, d_gate, d_up, d_weight, g_buf, select, part, part_in,
    in_sem, sib_send, sib_recv, z_send, z_recv, y_send, y_recv, g_send, g_recv,
    x_send, x_recv, a_send, a_recv, p_send, p_recv,
):
    y = lax.axis_index("dp")
    e = lax.axis_index("expert")
    x = lax.axis_index("tensor")
    z, c = e // 2, e % 2
    sib = (y, e + 1 - 2 * c, x)
    z_dev = lambda zz: (y, 2 * zz + c, x)
    y_dev = lambda k: ((y + k + 8) % 8, e, x)
    x_dev = lambda k: (y, e, (x + k + 4) % 4)
    m_me, h_me, p_me = (z // 2) % 4, z // 8, z % 2

    def remote(src, dst, send, recv, dev):
        return pltpu.make_async_remote_copy(
            src_ref=src, dst_ref=dst, send_sem=send, recv_sem=recv, device_id=dev, device_id_type=MESH
        )

    def landed(ref, sem):
        pltpu.make_async_copy(ref, ref, sem).wait()

    barrier = pltpu.get_barrier_semaphore()

    def greet(k, carry):
        pl.semaphore_signal(barrier, inc=1, device_id=z_dev((z + k) % 16), device_id_type=MESH)
        return carry

    for dev in (sib, y_dev(1), y_dev(-1), x_dev(1), x_dev(-1)):
        pl.semaphore_signal(barrier, inc=1, device_id=dev, device_id_type=MESH)
    lax.fori_loop(1, 16, greet, 0)

    loads = [
        (ids_in, ids), (probs_in, probs), (grad_in, xs.at[c]), (ddown_in, d_raw),
        (egate_in, e_gate), (eup_in, e_up), (dgate_in, d_gate), (dup_in, d_up),
    ] + [(edown_in.at[:, pl.ds(896 * k, 896)], weight.at[k]) for k in range(4)]
    loads = [pltpu.make_async_copy(s, d, in_sem.at[i]) for i, (s, d) in enumerate(loads)]
    for copy in loads:
        copy.start()

    loads[3].wait()
    d_weight[y, 0] = jnp.concatenate(
        [
            jnp.concatenate([d_raw[...].astype(F32), jnp.zeros((14, 32), F32)], axis=1),
            jnp.zeros((2, 640), F32),
        ],
        axis=0,
    ).astype(BF16)

    loads[0].wait()
    loads[1].wait()
    experts = iota((32, 128), 0)
    first, second = experts == ids[0:1, :], experts == ids[1:2, :]
    named = one_hot(first) + one_hot(second)
    earlier = nn(named, one_hot(iota((128, 128), 0) < iota((128, 128), 1)))
    cell_of = lambda j, hot: ids[j : j + 1, :].astype(F32) * 12.0 + jnp.sum(
        jnp.where(hot, earlier, 0.0), axis=0, keepdims=True
    )
    table[c] = jnp.concatenate(
        [cell_of(0, first), cell_of(1, second), probs[...], jnp.zeros((4, 128), F32)], axis=0
    )
    loads[2].wait()

    pl.semaphore_wait(barrier, 20)

    swap = [
        remote(table.at[c], table.at[c], sib_send.at[0], sib_recv.at[0], sib),
        remote(xs.at[c], xs.at[c], sib_send.at[1], sib_recv.at[1], sib),
    ]
    for copy in swap:
        copy.start()

    def z_step(s):
        plus = remote(
            d_weight.at[y, slot_of(1 - s)], d_weight.at[y, 15 if s == 8 else slot_of(-s)],
            z_send, z_recv.at[2 * s - 2], z_dev((z + 1) % 16),
        )
        plus.start()
        if s < 8:
            remote(
                d_weight.at[y, slot_of(s - 1)], d_weight.at[y, slot_of(s)],
                z_send, z_recv.at[2 * s - 1], z_dev((z + 15) % 16),
            ).start()

    def z_wait(s):
        landed(d_weight.at[y, 0], z_recv.at[2 * s - 2])
        if s < 8:
            landed(d_weight.at[y, 0], z_recv.at[2 * s - 1])

    z_step(1)

    q = iota((1, 512), 1)
    slot = (q >> 4) & 15
    half_off = (slot + 1) >> 1
    zq = (z + jnp.where((slot & 1) == 1, half_off, 16 - half_off)) & 15
    target = jnp.where((q & 15) < 14, (((q >> 8) * 16 + zq) * 2 + c) * 14 + (q & 15), -1)
    for k in range(7):
        select[pl.ds(128 * k, 128), :] = one_hot(iota((128, 512), 0) + 128 * k == target)

    for copy in swap:
        copy.wait_recv()

    w = iota((256, 1), 0)
    place = w & 15
    base = (2 * (w >> 4) + c) * 12
    target_a = jnp.where(place < 12, base + place, base + place - 12).astype(F32)
    target_b = (base + 4 + (place & 7)).astype(F32)

    def matched(core, wanted):
        tab = table[core]
        hit0, hit1 = tab[0:1, :] == wanted, tab[1:2, :] == wanted
        scale = jnp.sum(
            jnp.where(hit0, tab[2:3, :], 0.0) + jnp.where(hit1, tab[3:4, :], 0.0), axis=1, keepdims=True
        )
        return one_hot(hit0 | hit1), scale

    hot0, scale0 = matched(0, jnp.where(place < 12, target_a, -1.0))
    hot1, scale1 = matched(1, jnp.where(place >= 12, target_a, -1.0))
    sends[:, :, 0:896] = (
        ((nn(hot0, xs[0]) + nn(hot1, xs[1])) * (scale0 + scale1)).astype(BF16).reshape(16, 16, 896)
    )
    hot, scale = matched(1, target_b)
    rest = jnp.where(place < 8, nn(hot, xs[1, :, 0:512]), nn(hot, xs[1, :, 384:896]))
    sends[:, :, 896:1408] = (rest * scale).astype(BF16).reshape(16, 16, 512)

    def route(i):
        m = (m_me - i + 4) % 4
        if i == 0:
            own = pltpu.make_async_copy(sends.at[z], lands.at[h_me, m_me, p_me], a_recv.at[0])
            own.start()
            others = [(h_me, 1 - p_me), (1 - h_me, 0), (1 - h_me, 1)]
        else:
            others = [(0, 0), (1, 0), (0, 1), (1, 1)]
        for h, p in others:
            zz = h * 8 + m * 2 + p
            remote(
                sends.at[zz], lands.at[h_me, m_me, p_me], a_send, a_recv.at[i], z_dev(zz)
            ).start()

    for i in (0, 1, 3, 2):
        route(i)

    for s in range(2):
        g_buf[x, pl.ds(128 * s, 128), :] = nn(xs[s], select[...]).astype(BF16)

    def g_start():
        for k, sem in ((1, 0), (-1, 1)):
            remote(g_buf.at[x], g_buf.at[x], g_send, g_recv.at[sem], x_dev(k)).start()

    def g_forward():
        left, right = (x + 3) % 4, (x + 1) % 4
        landed(g_buf.at[0], g_recv.at[0])
        part_l = g_buf.at[left, pl.ds(0, 128)]
        remote(part_l, part_l, g_send, g_recv.at[2], x_dev(1)).start()
        landed(g_buf.at[0], g_recv.at[1])
        part_r = g_buf.at[right, pl.ds(128, 128)]
        remote(part_r, part_r, g_send, g_recv.at[3], x_dev(-1)).start()

    def g_wait():
        landed(g_buf.at[0, pl.ds(0, 128)], g_recv.at[2])
        landed(g_buf.at[0, pl.ds(0, 128)], g_recv.at[3])

    def y_index(g, j, plus):
        return 8 * g + 2 * (j - 1) + (0 if plus else 1)

    def y_steps(g, plus):
        return 4 if plus == (g % 2 == 0) else 3

    def y_step(g, j):
        a, b = Z_GROUPS[g]
        for plus in (True, False):
            if j <= y_steps(g, plus):
                origin = (y + (1 - j if plus else j - 1) + 8) % 8
                ref = d_weight.at[origin, pl.ds(a, b - a)]
                remote(ref, ref, y_send, y_recv.at[y_index(g, j, plus)], y_dev(1 if plus else -1)).start()

    def y_wait(g, j):
        a, b = Z_GROUPS[g]
        for plus in (True, False):
            if j <= y_steps(g, plus):
                landed(d_weight.at[0, pl.ds(a, b - a)], y_recv.at[y_index(g, j, plus)])

    qq = iota((96, 128), 0)
    ww = iota((96, 128), 1)
    chip = (
        jnp.where(qq >= 24, 1, 0) + jnp.where(qq >= 48, 1, 0) + jnp.where(qq >= 72, 1, 0)
    )
    row = qq - 24 * chip
    wrow = ww & 15
    same = ((ww >> 4) & 3) == chip
    head = same & (ww < 64) & (row == wrow)
    tail0 = same & (ww >= 64) & (row == wrow + 16) & (wrow < 8)
    tail1 = same & (ww >= 64) & (row == wrow + 8) & (wrow >= 8)
    pick0, pick1 = one_hot(head | tail0), one_hot(head | tail1)

    def group_of(i):
        return (m_me + i) % 4

    def gather_rows(i):
        m = group_of(i)
        landed(lands.at[:, 0], a_recv.at[i])
        got = jnp.concatenate([lands[0, m].reshape(32, 1408), lands[1, m].reshape(32, 1408)], axis=0)
        more = got[:, 896:1408]
        low = nn(pick0, jnp.concatenate([got[:, 0:512], more], axis=0))
        high = nn(pick1, jnp.concatenate([got[:, 512:896], more[:, 128:512]], axis=0))
        full = jnp.concatenate([low, high], axis=1).astype(BF16)
        rows[x, 0, m] = full[0:48]
        rows[x, 1, m] = full[48:96]
        ref = rows.at[x, :, m]
        remote(ref, ref, x_send, x_recv.at[4 * i], x_dev(1)).start()
        remote(ref, ref, x_send, x_recv.at[4 * i + 1], x_dev(-1)).start()

    def forward_rows(i):
        m = group_of(i)
        landed(rows.at[0, :, 0], x_recv.at[4 * i])
        part_l = rows.at[(x + 3) % 4, 0, m]
        remote(part_l, part_l, x_send, x_recv.at[4 * i + 2], x_dev(1)).start()
        landed(rows.at[0, :, 0], x_recv.at[4 * i + 1])
        part_r = rows.at[(x + 1) % 4, 1, m]
        remote(part_r, part_r, x_send, x_recv.at[4 * i + 3], x_dev(-1)).start()

    def end_rows(i):
        landed(rows.at[0, 0, 0], x_recv.at[4 * i + 2])
        landed(rows.at[0, 0, 0], x_recv.at[4 * i + 3])

    def expert_dot(k):
        return nt(weight[k], rows[k].reshape(384, 896))

    g_start()
    z_wait(1)
    z_step(2)
    y_step(0, 1)

    loads[4].wait()
    loads[5].wait()
    fac_gate[...], fac_up[...] = factors(e_gate[...], e_up[...])

    ready = {r: g for g, r in enumerate(Z_READY)}
    g_forward()
    actions = {3: [0], 6: [1], 8: [2]}
    for tick in range(2, 9):
        z_wait(tick)
        if tick < 8:
            z_step(tick + 1)
        if tick in ready:
            y_step(ready[tick], 1)
        for g in range(4):
            j = tick - Z_READY[g]
            if 1 <= j <= 4:
                y_wait(g, j)
                if j < 4:
                    y_step(g, j + 1)
        for i in actions.get(tick, ()):
            gather_rows(i)
            if i:
                forward_rows(i - 1)
    for tick in range(9, 13):
        for g in range(4):
            j = tick - Z_READY[g]
            if 1 <= j <= 4:
                y_wait(g, j)
                if j < 4:
                    y_step(g, j + 1)
        if tick == 9:
            gather_rows(3)
            forward_rows(2)
        if tick == 11:
            forward_rows(3)

    g_wait()
    total = jnp.zeros((256, 640), F32)
    for k in range(4):
        total += nn(g_buf[k], d_weight[2 * k : 2 * k + 2].reshape(512, 640))
    part[...] = total.reshape(2, 128, 640)
    give = remote(part.at[1 - c], part_in, p_send, p_recv, sib)
    give.start()

    for k in range(4):
        loads[8 + k].wait()
    acc[...] = expert_dot(x)

    loads[6].wait()
    loads[7].wait()
    gate_fac, up_fac = factors(d_gate[...], d_up[...])
    give.wait_recv()
    hidden = (part[c] + part_in[...]).T[0:608]
    dgate_out[...] = (hidden * gate_fac).astype(BF16)
    dup_out[...] = (hidden * up_fac).astype(BF16)

    acc[...] += expert_dot((x + 1) % 4)
    acc[...] += expert_dot((x + 3) % 4)
    for i in range(4):
        end_rows(i)
    hidden = acc[...] + expert_dot((x + 2) % 4)
    egate_out[...] = (hidden * fac_gate[...]).astype(BF16)
    eup_out[...] = (hidden * fac_up[...]).astype(BF16)

    for copy in swap:
        copy.wait_send()
    landed(d_weight.at[0, pl.ds(0, 15)], z_send)
    landed(d_weight.at[pl.ds(0, 7)], y_send)
    landed(g_buf.at[pl.ds(0, 3)], g_send)
    landed(rows.at[pl.ds(0, 3)], x_send)
    landed(sends.at[pl.ds(0, 15)], a_send)
    give.wait_send()


def local(
    out_grad, route_ids, route_probs, dense_gate_pre, dense_up_pre, dense_down,
    expert_gate_pre, expert_up_pre, expert_down,
):
    dma = pltpu.SemaphoreType.DMA
    vmem = pltpu.VMEM
    shapes = [
        vmem((2, 128), jnp.int32), vmem((2, 128), F32), vmem((2, 8, 128), F32),
        vmem((2, 128, 896), BF16), vmem((16, 16, 1408), BF16), vmem((2, 4, 2, 16, 1408), BF16),
        vmem((4, 2, 4, 48, 896), BF16), vmem((4, 608, 896), BF16), vmem((608, 384), F32),
        vmem((608, 384), BF16), vmem((608, 384), BF16), vmem((608, 384), F32), vmem((608, 384), F32),
        vmem((14, 608), BF16), vmem((608, 128), BF16), vmem((608, 128), BF16),
        vmem((8, 16, 16, 640), BF16), vmem((4, 256, 512), BF16), vmem((896, 512), BF16),
        vmem((2, 128, 640), F32), vmem((128, 640), F32),
        dma((12,)), dma((2,)), dma((2,)), dma, dma((15,)), dma, dma((32,)), dma, dma((4,)),
        dma, dma((16,)), dma, dma((4,)), dma, dma,
    ]
    any_spec = pl.BlockSpec(memory_space=pl.ANY)
    whole = pl.BlockSpec(memory_space=pltpu.VMEM)
    dgate, dup, egate, eup = pl.pallas_call(
        kernel,
        out_shape=[
            jax.ShapeDtypeStruct((608, 128), BF16), jax.ShapeDtypeStruct((608, 128), BF16),
            jax.ShapeDtypeStruct((608, 384), BF16), jax.ShapeDtypeStruct((608, 384), BF16),
        ],
        in_specs=[any_spec] * 9,
        out_specs=[whole] * 4,
        scratch_shapes=shapes,
        compiler_params=pltpu.CompilerParams(
            collective_id=0, has_side_effects=True, vmem_limit_bytes=48 << 20
        ),
        cost_estimate=pl.CostEstimate(
            flops=2 * 512 * 608 * 3584, bytes_accessed=8 << 20, transcendentals=512 * 608
        ),
    )(
        out_grad, route_ids.T, route_probs.T, dense_gate_pre.T, dense_up_pre.T, dense_down.T,
        expert_gate_pre[0, 0].T, expert_up_pre[0, 0].T, expert_down[0],
    )
    return (
        dgate.T, dup.T, egate.T.reshape(expert_gate_pre.shape), eup.T.reshape(expert_up_pre.shape),
    )


def solution(mesh):
    placed = (
        P(("dp", "expert"), "tensor"),
        P(("dp", "expert"), None),
        P(("dp", "expert"), None),
        P(("dp", "expert"), "tensor"),
        P(("dp", "expert"), "tensor"),
        P("tensor", ("dp", "expert")),
        P("dp", "expert", None, "tensor"),
        P("dp", "expert", None, "tensor"),
        P("expert", "tensor", None),
    )
    return jax.shard_map(
        local,
        mesh=mesh,
        in_specs=placed,
        out_specs=(
            P(("dp", "expert"), "tensor"),
            P(("dp", "expert"), "tensor"),
            P("dp", "expert", None, "tensor"),
            P("dp", "expert", None, "tensor"),
        ),
        check_vma=False,
    )
```

time: 299 us -> 117 us (0.39)
  waiting for transfers between devices: 173 us -> 0 us
  Pallas kernels: 0 us -> 106 us
  blocking collectives: 83.1 us -> 0 us
  between operations: 14.2 us -> 0.66 us
  matrix products: 11.6 us -> 0 us
  local copies, waits for them, and re-layouts: 14.6 us -> 9.75 us
    all_gather x2 -> x0, waiting for transfers between devices: 172 us -> none  [the longest x1 148 us: local(): lax.all_gather(dense_down, ('dp', 'expert'), axis=1, tiled=True)]
    pallas_call x0 -> x1, Pallas kernels: none -> 106 us  [local(): pl.pallas_call(kernel, out_shape=[jax.ShapeDtypeStruct((608, 128), BF16),...]
    all_to_all x1 -> x0, blocking collectives: 70.4 us -> none  [local(): lax.all_to_all(sent_rows, 'expert', split_axis=0, concat_axis=0, tiled=True)]
    all_gather x1 -> x0, blocking collectives: 12.7 us -> none  [local(): full_grad = lax.all_gather(out_grad, 'tensor', axis=1, tiled=True)]
    dot_general x2 -> x0, matrix products: 11.6 us -> none  [the longest x1 6.66 us: local(): lax.dot_general(lax.all_gather(arrived, 'tensor', axis=1, tiled=True), we...]
    unnamed x13 -> x20, local copies, waits for them, and re-layouts: 10.2 us -> 9.75 us
  transfers between devices with their start and end apart: 2 -> 0, of which waited for: 2 -> 0; matrix products, arithmetic and copies ran while one was open for 2% -> 0% of each run, Pallas kernels for 0% -> 0%
where the time goes in v1:
time: 117 us; the launch traced here: 116 us
  Pallas kernels  106 us (91%)
  local copies, waits for them, and re-layouts  9.75 us (8%)
    pallas_call x1, Pallas kernels, local(): pl.pallas_call(kernel, out_shape=[jax.ShapeDtypeStruct((608, 128), BF16),...  106 us
    unnamed x20, local copies, waits for them, and re-layouts  9.75 us

profile of v1, /device:TPU:1, one launch (start us, length us, event | category | flops | bytes accessed | tf_op | source)
XLA Modules:
  0.0 116.3 jit_solution(4154288240784834539)
XLA Ops:
  0.6 0.0 copy-start
  0.6 1.0 copy-done
  1.7 0.0 copy-start.1
  1.7 1.0 copy-done.1
  2.7 0.0 copy-start.2
  2.7 0.9 copy-done.2
  3.6 0.0 copy-start.3
  3.6 0.9 copy-done.3
  4.5 0.0 copy-start.4
  4.5 0.9 copy-done.4
  5.4 0.0 copy-start.5
  5.4 0.7 copy-done.5
  6.2 0.0 copy-start.6
  6.2 0.7 copy-done.6
  6.9 0.0 copy-start.7
  6.9 0.7 copy-done.7
  7.5 105.9 %shard_map.120 = (bf16[608,128]{1,0:T(8,128)(2,1)S(1)}, bf16[608,128]{1,0:T(8,128)(2,1)S(1)}, bf16[608,384]{1,0:T(8,128)(2,1)S(1)}, bf16[608,384]{1,0:T(8,128)(2,1)S(1)}) custom-call(bf16[128,896]{1,0:T(8,128)(2,1)S(1)} %copy-done.2, s32[2,128]{1,0:T(2,128)S(1)} %bitcast.29, f32[2,128]{1,0:T(2,128)S(1)} %bitcast.30, bf16[608,128]{1,0:T(8,128)(2,1)S(1)} %bitcast.26, ...), custom_call_target="tpu_custom_call" | custom-call | flops 2231369728 | bytes 8388608 | tf_op jit(solution)/shard_map/pallas_call | solution.py:377
  113.4 0.7 copy.17
  114.1 0.7 copy.18
  114.8 0.8 copy.19
  115.5 0.8 copy.20
Async XLA Ops:
  0.6 1.0 copy-start
  1.7 1.0 copy-start.1
  2.7 0.9 copy-start.2
  3.6 0.9 copy-start.3
  4.5 0.9 copy-start.4
  5.4 0.7 copy-start.5
  6.2 0.7 copy-start.6
  6.9 0.7 copy-start.7

commit v2 on v1

--- a/solution.py
+++ b/solution.py
@@ -13,6 +13,10 @@
 
 Z_GROUPS = ((0, 3), (3, 7), (7, 11), (11, 16))
 Z_READY = (1, 3, 5, 8)
+Y_TICKS = {
+    4: ((0, 1),), 6: ((0, 2),), 7: ((1, 1),), 8: ((0, 3),), 9: ((1, 2), (2, 1)), 10: ((0, 4),),
+    11: ((1, 3), (2, 2), (3, 1)), 12: ((1, 4),), 13: ((2, 3), (3, 2)), 14: ((2, 4), (3, 3)), 15: ((3, 4),),
+}
 
 
 def slot_of(offset):
@@ -60,7 +64,7 @@
     z_dev = lambda zz: (y, 2 * zz + c, x)
     y_dev = lambda k: ((y + k + 8) % 8, e, x)
     x_dev = lambda k: (y, e, (x + k + 4) % 4)
-    m_me, h_me, p_me = (z // 2) % 4, z // 8, z % 2
+    pair, half = z // 2, z % 2
 
     def remote(src, dst, send, recv, dev):
         return pltpu.make_async_remote_copy(
@@ -147,6 +151,8 @@
     for k in range(7):
         select[pl.ds(128 * k, 128), :] = one_hot(iota((128, 512), 0) + 128 * k == target)
 
+    z_wait(1)
+    z_step(2)
     for copy in swap:
         copy.wait_recv()
 
@@ -169,29 +175,24 @@
     sends[:, :, 0:896] = (
         ((nn(hot0, xs[0]) + nn(hot1, xs[1])) * (scale0 + scale1)).astype(BF16).reshape(16, 16, 896)
     )
+    z_wait(2)
+    z_step(3)
     hot, scale = matched(1, target_b)
     rest = jnp.where(place < 8, nn(hot, xs[1, :, 0:512]), nn(hot, xs[1, :, 384:896]))
     sends[:, :, 896:1408] = (rest * scale).astype(BF16).reshape(16, 16, 512)
 
+    def group_of(i):
+        return (pair + i) % 8, (pair + (4 if i == 0 else 8 - i)) % 8
+
     def route(i):
-        m = (m_me - i + 4) % 4
+        near, far = group_of(i)
+        spots = [(near, 0), (near, 1), (far, 0), (far, 1)]
         if i == 0:
-            own = pltpu.make_async_copy(sends.at[z], lands.at[h_me, m_me, p_me], a_recv.at[0])
-            own.start()
-            others = [(h_me, 1 - p_me), (1 - h_me, 0), (1 - h_me, 1)]
-        else:
-            others = [(0, 0), (1, 0), (0, 1), (1, 1)]
-        for h, p in others:
-            zz = h * 8 + m * 2 + p
-            remote(
-                sends.at[zz], lands.at[h_me, m_me, p_me], a_send, a_recv.at[i], z_dev(zz)
-            ).start()
-
-    for i in (0, 1, 3, 2):
-        route(i)
-
-    for s in range(2):
-        g_buf[x, pl.ds(128 * s, 128), :] = nn(xs[s], select[...]).astype(BF16)
+            pltpu.make_async_copy(sends.at[z], lands.at[pair, half], a_recv.at[0]).start()
+            spots = [(near, 1 - half)] + spots[2:]
+        for m, p in spots:
+            zz = m * 2 + p
+            remote(sends.at[zz], lands.at[pair, half], a_send, a_recv.at[i], z_dev(zz)).start()
 
     def g_start():
         for k, sem in ((1, 0), (-1, 1)):
@@ -213,22 +214,22 @@
     def y_index(g, j, plus):
         return 8 * g + 2 * (j - 1) + (0 if plus else 1)
 
-    def y_steps(g, plus):
-        return 4 if plus == (g % 2 == 0) else 3
+    def y_span(g, j, plus):
+        a, b = Z_GROUPS[g]
+        mid = (a + b + g % 2) // 2
+        return (a, b) if j < 4 else ((a, mid) if plus else (mid, b))
 
     def y_step(g, j):
-        a, b = Z_GROUPS[g]
         for plus in (True, False):
-            if j <= y_steps(g, plus):
-                origin = (y + (1 - j if plus else j - 1) + 8) % 8
-                ref = d_weight.at[origin, pl.ds(a, b - a)]
-                remote(ref, ref, y_send, y_recv.at[y_index(g, j, plus)], y_dev(1 if plus else -1)).start()
+            a, b = y_span(g, j, plus)
+            origin = (y + (1 - j if plus else j - 1) + 8) % 8
+            ref = d_weight.at[origin, pl.ds(a, b - a)]
+            remote(ref, ref, y_send, y_recv.at[y_index(g, j, plus)], y_dev(1 if plus else -1)).start()
 
     def y_wait(g, j):
-        a, b = Z_GROUPS[g]
         for plus in (True, False):
-            if j <= y_steps(g, plus):
-                landed(d_weight.at[0, pl.ds(a, b - a)], y_recv.at[y_index(g, j, plus)])
+            a, b = y_span(g, j, plus)
+            landed(d_weight.at[0, pl.ds(a, b - a)], y_recv.at[y_index(g, j, plus)])
 
     qq = iota((96, 128), 0)
     ww = iota((96, 128), 1)
@@ -243,79 +244,81 @@
     tail1 = same & (ww >= 64) & (row == wrow + 8) & (wrow >= 8)
     pick0, pick1 = one_hot(head | tail0), one_hot(head | tail1)
 
-    def group_of(i):
-        return (m_me + i) % 4
-
     def gather_rows(i):
-        m = group_of(i)
-        landed(lands.at[:, 0], a_recv.at[i])
-        got = jnp.concatenate([lands[0, m].reshape(32, 1408), lands[1, m].reshape(32, 1408)], axis=0)
+        blocks = group_of(i)
+        landed(lands.at[pl.ds(0, 2)], a_recv.at[i])
+        got = jnp.concatenate([lands[m].reshape(32, 1408) for m in blocks], axis=0)
         more = got[:, 896:1408]
         low = nn(pick0, jnp.concatenate([got[:, 0:512], more], axis=0))
         high = nn(pick1, jnp.concatenate([got[:, 512:896], more[:, 128:512]], axis=0))
         full = jnp.concatenate([low, high], axis=1).astype(BF16)
-        rows[x, 0, m] = full[0:48]
-        rows[x, 1, m] = full[48:96]
-        ref = rows.at[x, :, m]
-        remote(ref, ref, x_send, x_recv.at[4 * i], x_dev(1)).start()
-        remote(ref, ref, x_send, x_recv.at[4 * i + 1], x_dev(-1)).start()
+        for k, m in enumerate(blocks):
+            rows[x, m] = full[48 * k : 48 * k + 48]
+        for m in blocks:
+            ref = rows.at[x, m]
+            remote(ref, ref, x_send, x_recv.at[4 * i], x_dev(1)).start()
+            remote(ref, ref, x_send, x_recv.at[4 * i + 1], x_dev(-1)).start()
 
     def forward_rows(i):
-        m = group_of(i)
-        landed(rows.at[0, :, 0], x_recv.at[4 * i])
-        part_l = rows.at[(x + 3) % 4, 0, m]
+        near, far = group_of(i)
+        landed(rows.at[0, pl.ds(0, 2)], x_recv.at[4 * i])
+        part_l = rows.at[(x + 3) % 4, near]
         remote(part_l, part_l, x_send, x_recv.at[4 * i + 2], x_dev(1)).start()
-        landed(rows.at[0, :, 0], x_recv.at[4 * i + 1])
-        part_r = rows.at[(x + 1) % 4, 1, m]
+        landed(rows.at[0, pl.ds(0, 2)], x_recv.at[4 * i + 1])
+        part_r = rows.at[(x + 1) % 4, far]
         remote(part_r, part_r, x_send, x_recv.at[4 * i + 3], x_dev(-1)).start()
 
     def end_rows(i):
-        landed(rows.at[0, 0, 0], x_recv.at[4 * i + 2])
-        landed(rows.at[0, 0, 0], x_recv.at[4 * i + 3])
+        landed(rows.at[0, 0], x_recv.at[4 * i + 2])
+        landed(rows.at[0, 0], x_recv.at[4 * i + 3])
 
     def expert_dot(k):
         return nt(weight[k], rows[k].reshape(384, 896))
 
+    def tick(t):
+        if t <= 8:
+            z_wait(t)
+            if t < 8:
+                z_step(t + 1)
+            if t in Z_READY:
+                y_step(Z_READY.index(t), 1)
+        for g, j in Y_TICKS.get(t, ()):
+            y_wait(g, j)
+            if j < 4:
+                y_step(g, j + 1)
+
+    y_step(0, 1)
+    route(3)
+    for t in (3, 4):
+        tick(t)
+    route(2)
+    for s in range(2):
+        g_buf[x, pl.ds(128 * s, 128), :] = nn(xs[s], select[...]).astype(BF16)
     g_start()
-    z_wait(1)
-    z_step(2)
-    y_step(0, 1)
+    for t in (5, 6, 7, 8):
+        tick(t)
+    route(0)
 
     loads[4].wait()
     loads[5].wait()
     fac_gate[...], fac_up[...] = factors(e_gate[...], e_up[...])
-
-    ready = {r: g for g, r in enumerate(Z_READY)}
     g_forward()
-    actions = {3: [0], 6: [1], 8: [2]}
-    for tick in range(2, 9):
-        z_wait(tick)
-        if tick < 8:
-            z_step(tick + 1)
-        if tick in ready:
-            y_step(ready[tick], 1)
-        for g in range(4):
-            j = tick - Z_READY[g]
-            if 1 <= j <= 4:
-                y_wait(g, j)
-                if j < 4:
-                    y_step(g, j + 1)
-        for i in actions.get(tick, ()):
-            gather_rows(i)
-            if i:
-                forward_rows(i - 1)
-    for tick in range(9, 13):
-        for g in range(4):
-            j = tick - Z_READY[g]
-            if 1 <= j <= 4:
-                y_wait(g, j)
-                if j < 4:
-                    y_step(g, j + 1)
-        if tick == 9:
-            gather_rows(3)
-            forward_rows(2)
-        if tick == 11:
-            forward_rows(3)
+    for t in (9,):
+        tick(t)
+    gather_rows(3)
+    route(1)
+    for t in (10, 11,):
+        tick(t)
+    forward_rows(3)
+    gather_rows(2)
+    for t in (12,):
+        tick(t)
+    for t in (13, 14):
+        tick(t)
+    forward_rows(2)
+    gather_rows(0)
+    for t in (15,):
+        tick(t)
 
     g_wait()
     total = jnp.zeros((256, 640), F32)
@@ -324,11 +327,14 @@
     part[...] = total.reshape(2, 128, 640)
     give = remote(part.at[1 - c], part_in, p_send, p_recv, sib)
     give.start()
+    gather_rows(1)
+    forward_rows(0)
 
     for k in range(4):
         loads[8 + k].wait()
     acc[...] = expert_dot(x)
 
+    forward_rows(1)
     loads[6].wait()
     loads[7].wait()
     gate_fac, up_fac = factors(d_gate[...], d_up[...])
@@ -337,8 +343,7 @@
     dgate_out[...] = (hidden * gate_fac).astype(BF16)
     dup_out[...] = (hidden * up_fac).astype(BF16)
 
-    acc[...] += expert_dot((x + 1) % 4)
-    acc[...] += expert_dot((x + 3) % 4)
+    acc[...] += expert_dot((x + 1) % 4) + expert_dot((x + 3) % 4)
     for i in range(4):
         end_rows(i)
     hidden = acc[...] + expert_dot((x + 2) % 4)
@@ -363,8 +368,8 @@
     vmem = pltpu.VMEM
     shapes = [
         vmem((2, 128), jnp.int32), vmem((2, 128), F32), vmem((2, 8, 128), F32),
-        vmem((2, 128, 896), BF16), vmem((16, 16, 1408), BF16), vmem((2, 4, 2, 16, 1408), BF16),
-        vmem((4, 2, 4, 48, 896), BF16), vmem((4, 608, 896), BF16), vmem((608, 384), F32),
+        vmem((2, 128, 896), BF16), vmem((16, 16, 1408), BF16), vmem((8, 2, 16, 1408), BF16),
+        vmem((4, 8, 48, 896), BF16), vmem((4, 608, 896), BF16), vmem((608, 384), F32),
         vmem((608, 384), BF16), vmem((608, 384), BF16), vmem((608, 384), F32), vmem((608, 384), F32),
         vmem((14, 608), BF16), vmem((608, 128), BF16), vmem((608, 128), BF16),
         vmem((8, 16, 16, 640), BF16), vmem((4, 256, 512), BF16), vmem((896, 512), BF16),
@@ -372,7 +377,7 @@
         dma((12,)), dma((2,)), dma((2,)), dma, dma((15,)), dma, dma((32,)), dma, dma((4,)),
         dma, dma((16,)), dma, dma((4,)), dma, dma,
     ]
-    any_spec = pl.BlockSpec(memory_space=pl.ANY)
+    any_spec = pl.BlockSpec(memory_space=pltpu.HBM)
     whole = pl.BlockSpec(memory_space=pltpu.VMEM)
     dgate, dup, egate, eup = pl.pallas_call(
         kernel,
@@ -384,7 +389,7 @@
         out_specs=[whole] * 4,
         scratch_shapes=shapes,
         compiler_params=pltpu.CompilerParams(
-            collective_id=0, has_side_effects=True, vmem_limit_bytes=48 << 20
+            collective_id=0, has_side_effects=True, vmem_limit_bytes=62 << 20
         ),
         cost_estimate=pl.CostEstimate(
             flops=2 * 512 * 608 * 3584, bytes_accessed=8 << 20, transcendentals=512 * 608

time: 117 us -> 102 us (0.87)
  the two profiles are of different devices: /device:TPU:1 before, /device:TPU:2 now
where the time goes in v2:
time: 102 us; the launch traced here: 101 us
  Pallas kernels  93.7 us (92%)
  local copies, waits for them, and re-layouts  6.85 us (7%)
    pallas_call x1, Pallas kernels, local(): pl.pallas_call(kernel, out_shape=[jax.ShapeDtypeStruct((608, 128), BF16),...  93.7 us
    unnamed x4, local copies, waits for them, and re-layouts  6.85 us

profile of v2, /device:TPU:2, one launch (start us, length us, event | category | flops | bytes accessed | tf_op | source)
XLA Modules:
  0.0 101.2 jit_solution(1928011922752096261)
XLA Ops:
  0.6 93.7 %shard_map.120 = (bf16[608,128]{1,0:T(8,128)(2,1)}, bf16[608,128]{1,0:T(8,128)(2,1)}, bf16[608,384]{1,0:T(8,128)(2,1)}, bf16[608,384]{1,0:T(8,128)(2,1)}) custom-call(bf16[128,896]{1,0:T(8,128)(2,1)} %grad_in.1, s32[2,128]{1,0:T(2,128)} %bitcast.30, f32[2,128]{1,0:T(2,128)} %bitcast.31, bf16[608,128]{1,0:T(8,128)(2,1)} %bitcast.27, ...), custom_call_target="tpu_custom_call" | custom-call | flops 2231369728 | bytes 8388608 | tf_op jit(solution)/shard_map/pallas_call | solution.py:382
  94.4 1.6 %copy.17 = bf16[128,608]{0,1:T(8,128)(2,1)} copy(bf16[128,608]{0,1:T(8,128)(2,1)} %bitcast.23) | data formatting | bytes 311296
  96.0 1.6 %copy.18 = bf16[128,608]{0,1:T(8,128)(2,1)} copy(bf16[128,608]{0,1:T(8,128)(2,1)} %bitcast.22) | data formatting | bytes 311296
  97.6 1.8 %copy.19 = bf16[1,1,384,608]{2,3,1,0:T(8,128)(2,1)} copy(bf16[1,1,384,608]{2,3,1,0:T(8,128)(2,1)} %bitcast.21) | data formatting | bytes 933888
  99.4 1.8 %copy.20 = bf16[1,1,384,608]{2,3,1,0:T(8,128)(2,1)} copy(bf16[1,1,384,608]{2,3,1,0:T(8,128)(2,1)} %bitcast.20) | data formatting | bytes 933888

commit v3 on v2

--- a/solution.py
+++ b/solution.py
@@ -288,37 +288,37 @@
                 y_step(g, j + 1)
 
     y_step(0, 1)
-    route(3)
+    route(1)
     for t in (3, 4):
         tick(t)
-    route(2)
+    route(0)
     for s in range(2):
         g_buf[x, pl.ds(128 * s, 128), :] = nn(xs[s], select[...]).astype(BF16)
     g_start()
     for t in (5, 6, 7, 8):
         tick(t)
-    route(0)
+    route(2)
 
     loads[4].wait()
     loads[5].wait()
     fac_gate[...], fac_up[...] = factors(e_gate[...], e_up[...])
     g_forward()
-    for t in (9,):
-        tick(t)
+    tick(9)
+    gather_rows(1)
+    route(3)
+    tick(10)
+    tick(11)
+    forward_rows(1)
+    gather_rows(0)
+    tick(12)
+    forward_rows(0)
+    gather_rows(2)
+    tick(13)
     gather_rows(3)
-    route(1)
-    for t in (10, 11,):
-        tick(t)
+    forward_rows(2)
+    tick(14)
     forward_rows(3)
-    gather_rows(2)
-    for t in (12,):
-        tick(t)
-    for t in (13, 14):
-        tick(t)
-    forward_rows(2)
-    gather_rows(0)
-    for t in (15,):
-        tick(t)
+    tick(15)
 
     g_wait()
     total = jnp.zeros((256, 640), F32)
@@ -327,14 +327,10 @@
     part[...] = total.reshape(2, 128, 640)
     give = remote(part.at[1 - c], part_in, p_send, p_recv, sib)
     give.start()
-    gather_rows(1)
-    forward_rows(0)
-
     for k in range(4):
         loads[8 + k].wait()
     acc[...] = expert_dot(x)
-
-    forward_rows(1)
+    acc[...] += expert_dot((x + 1) % 4) + expert_dot((x + 3) % 4)
     loads[6].wait()
     loads[7].wait()
     gate_fac, up_fac = factors(d_gate[...], d_up[...])
@@ -343,7 +339,6 @@
     dgate_out[...] = (hidden * gate_fac).astype(BF16)
     dup_out[...] = (hidden * up_fac).astype(BF16)
 
-    acc[...] += expert_dot((x + 1) % 4) + expert_dot((x + 3) % 4)
     for i in range(4):
         end_rows(i)
     hidden = acc[...] + expert_dot((x + 2) % 4)

time: 102 us -> 93.2 us (0.914)
  the two profiles are of different devices: /device:TPU:2 before, /device:TPU:1 now
where the time goes in v3:
time: 93.2 us; the launch traced here: 91.8 us
  Pallas kernels  84.3 us (90%)
  local copies, waits for them, and re-layouts  6.85 us (7%)
    pallas_call x1, Pallas kernels, local(): pl.pallas_call(kernel, out_shape=[jax.ShapeDtypeStruct((608, 128), BF16),...  84.3 us
    unnamed x4, local copies, waits for them, and re-layouts  6.85 us

profile of v3, /device:TPU:1, one launch (start us, length us, event | category | flops | bytes accessed | tf_op | source)
XLA Modules:
  0.0 91.8 jit_solution(14383103946973110160)
XLA Ops:
  0.6 84.3 %shard_map.120 = (bf16[608,128]{1,0:T(8,128)(2,1)}, bf16[608,128]{1,0:T(8,128)(2,1)}, bf16[608,384]{1,0:T(8,128)(2,1)}, bf16[608,384]{1,0:T(8,128)(2,1)}) custom-call(bf16[128,896]{1,0:T(8,128)(2,1)} %grad_in.1, s32[2,128]{1,0:T(2,128)} %bitcast.30, f32[2,128]{1,0:T(2,128)} %bitcast.31, bf16[608,128]{1,0:T(8,128)(2,1)} %bitcast.27, ...), custom_call_target="tpu_custom_call" | custom-call | flops 2231369728 | bytes 8388608 | tf_op jit(solution)/shard_map/pallas_call | solution.py:377
  84.9 1.6 %copy.17 = bf16[128,608]{0,1:T(8,128)(2,1)} copy(bf16[128,608]{0,1:T(8,128)(2,1)} %bitcast.23) | data formatting | bytes 311296
  86.5 1.6 %copy.18 = bf16[128,608]{0,1:T(8,128)(2,1)} copy(bf16[128,608]{0,1:T(8,128)(2,1)} %bitcast.22) | data formatting | bytes 311296
  88.1 1.8 %copy.19 = bf16[1,1,384,608]{2,3,1,0:T(8,128)(2,1)} copy(bf16[1,1,384,608]{2,3,1,0:T(8,128)(2,1)} %bitcast.21) | data formatting | bytes 933888
  90.0 1.8 %copy.20 = bf16[1,1,384,608]{2,3,1,0:T(8,128)(2,1)} copy(bf16[1,1,384,608]{2,3,1,0:T(8,128)(2,1)} %bitcast.20) | data formatting | bytes 933888
